TPU v7x, 32 devices: a whole 2x2x4 slice. The times are simulated.
32 devices in a mesh: dp: 8 (over z, y), expert: 4 (over x, core).
Axes of the slice: x: 2, y: 2, z: 4, core: 2. Of those that a mesh axis runs over, the one named last changes fastest.
Arguments:
- tokens: bfloat16 [4096, 2048], P(('dp', 'expert')), may hold values from -6 to 6
- routes: int32 [4096, 4], P(('dp', 'expert')), may hold values from 0 to 7, all different within a row; in each aligned block of 128 rows (0 to 127, 128 to 255, ...) at most 96 rows name the same one
- combine: bfloat16 [4096, 4], P(('dp', 'expert')), may hold values from 0.049804688 to 1
- out_cotangent: bfloat16 [4096, 2048], P(('dp', 'expert')), may hold values from -1.5 to 1.5
- gate_weight: bfloat16 [8, 2048, 384], P('expert'), may hold values from -0.125 to 0.125
- up_weight: bfloat16 [8, 2048, 384], P('expert'), may hold values from -0.125 to 0.125
- down_weight: bfloat16 [8, 2048, 384], P('expert'), may hold values from -0.3125 to 0.3125
Outputs:
- token_grads: bfloat16 [4096, 2048], P(('dp', 'expert'))
- combine_grads: bfloat16 [4096, 4], P(('dp', 'expert'))
- gate_grads: float32 [8, 2048, 384], P('expert', 'dp')
- up_grads: float32 [8, 2048, 384], P('expert', 'dp')
- down_grads: float32 [8, 2048, 384], P('expert', 'dp')
Inputs may be any that keep to these rules, and one draw needn't show every extreme that they name: `routes`: each token names 4 different experts; among the 128 tokens of one device no expert is named more than 96 times, and in some devices an expert is named exactly 96 times.
All inputs are finite; a program needn't handle non-finite values.
Results may differ from a plain program's by a relative error of at most 0.017.
Values may be sent and summed in bfloat16 or wider, within the bound.
A program may use at most 128 MiB of HBM per device.

v0:
```python
import jax
import jax.numpy as jnp
from jax import lax
from jax.sharding import PartitionSpec as P


def slot_of_route(routes, experts, capacity):
    flat_ids = routes.reshape(-1)
    onehot = (flat_ids[:, None] == jnp.arange(experts, dtype=jnp.int32)[None, :]).astype(jnp.int32)
    before = jnp.cumsum(onehot, axis=0) - onehot
    return flat_ids * capacity + jnp.sum(before * onehot, axis=1)


def local(tokens, routes, combine, out_cotangent, gate_weight, up_weight, down_weight):
    tok_local, model_width = tokens.shape
    top_k = routes.shape[1]
    expert_ranks = lax.axis_size("expert")
    exp_local = gate_weight.shape[0]
    experts = expert_ranks * exp_local
    capacity = 3 * tok_local * top_k // (2 * experts)
    routed = tok_local * top_k
    slot_ids = slot_of_route(routes, experts, capacity)
    owner_ids = (
        jnp.full((experts * capacity,), routed, jnp.int32)
        .at[slot_ids]
        .set(jnp.arange(routed, dtype=jnp.int32))
    )
    source_rows = owner_ids // top_k
    zero_row = jnp.zeros((1, model_width), jnp.bfloat16)
    token_pad = jnp.concatenate([tokens, zero_row], 0)
    cot_pad = jnp.concatenate([out_cotangent, zero_row], 0)
    weight_pad = jnp.concatenate([combine.reshape(-1), jnp.zeros((1,), jnp.bfloat16)], 0)
    layout = (expert_ranks, exp_local, capacity)
    sent_rows = token_pad[source_rows].reshape(layout + (model_width,))
    slot_weight = weight_pad[owner_ids]
    token_rows = lax.all_to_all(sent_rows, "expert", split_axis=0, concat_axis=0, tiled=True)
    gate_act = jnp.einsum(
        "secd,edf->secf", token_rows, gate_weight, preferred_element_type=jnp.float32
    )
    up_act = jnp.einsum("secd,edf->secf", token_rows, up_weight, preferred_element_type=jnp.float32)
    gate_sig = jax.nn.sigmoid(gate_act)
    hidden = (gate_act * gate_sig * up_act).astype(jnp.bfloat16)
    expert_out = jnp.einsum(
        "secf,edf->secd", hidden, down_weight, preferred_element_type=jnp.float32
    ).astype(jnp.bfloat16)
    token_rows, gate_act, gate_sig, up_act, hidden, expert_out = (
        token_rows,
        gate_act,
        gate_sig,
        up_act,
        hidden,
        expert_out,
    )
    returned = lax.all_to_all(expert_out, "expert", split_axis=0, concat_axis=0, tiled=True)
    picked = returned.reshape(experts * capacity, model_width)[slot_ids].reshape(
        tok_local, top_k, model_width
    )
    combine_grads = jnp.einsum(
        "tkd,td->tk", picked, out_cotangent, preferred_element_type=jnp.float32
    ).astype(jnp.bfloat16)
    cot_rows = cot_pad[source_rows]
    weighted = (slot_weight.astype(jnp.float32)[:, None] * cot_rows.astype(jnp.float32)).astype(
        jnp.bfloat16
    )
    out_cot = lax.all_to_all(
        weighted.reshape(layout + (model_width,)), "expert", split_axis=0, concat_axis=0, tiled=True
    )
    hidden_cot = jnp.einsum(
        "secd,edf->secf", out_cot, down_weight, preferred_element_type=jnp.float32
    )
    gate_cot = (hidden_cot * up_act * gate_sig * (1.0 + gate_act * (1.0 - gate_sig))).astype(
        jnp.bfloat16
    )
    up_cot = (hidden_cot * gate_act * gate_sig).astype(jnp.bfloat16)
    down_terms = jnp.einsum("secd,secf->edf", out_cot, hidden, preferred_element_type=jnp.float32)
    gate_terms = jnp.einsum(
        "secd,secf->edf", token_rows, gate_cot, preferred_element_type=jnp.float32
    )
    up_terms = jnp.einsum("secd,secf->edf", token_rows, up_cot, preferred_element_type=jnp.float32)
    rows_cot = (
        jnp.einsum("secf,edf->secd", gate_cot, gate_weight, preferred_element_type=jnp.float32)
        + jnp.einsum("secf,edf->secd", up_cot, up_weight, preferred_element_type=jnp.float32)
    ).astype(jnp.bfloat16)
    dgrad_rows = lax.all_to_all(rows_cot, "expert", split_axis=0, concat_axis=0, tiled=True)
    gathered = dgrad_rows.reshape(experts * capacity, model_width)[slot_ids].reshape(
        tok_local, top_k, model_width
    )
    token_grads = jnp.sum(gathered, axis=1, dtype=jnp.float32).astype(jnp.bfloat16)
    gate_grads, up_grads, down_grads = (
        lax.psum_scatter(
            gate_terms.astype(jnp.bfloat16), "dp", scatter_dimension=1, tiled=True
        ).astype(jnp.float32),
        lax.psum_scatter(
            up_terms.astype(jnp.bfloat16), "dp", scatter_dimension=1, tiled=True
        ).astype(jnp.float32),
        lax.psum_scatter(
            down_terms.astype(jnp.bfloat16), "dp", scatter_dimension=1, tiled=True
        ).astype(jnp.float32),
    )
    return (token_grads, combine_grads, gate_grads, up_grads, down_grads)


def solution(mesh):
    return jax.shard_map(
        local,
        mesh=mesh,
        in_specs=(
            P(("dp", "expert"), None),
            P(("dp", "expert"), None),
            P(("dp", "expert"), None),
            P(("dp", "expert"), None),
            P("expert", None, None),
            P("expert", None, None),
            P("expert", None, None),
        ),
        out_specs=(
            P(("dp", "expert"), None),
            P(("dp", "expert"), None),
            P("expert", "dp", None),
            P("expert", "dp", None),
            P("expert", "dp", None),
        ),
        check_vma=False,
    )
```

profile of v0, /device:TPU:0, one launch (start us, length us, event | category | flops | bytes accessed | tf_op | source)
XLA Modules:
  0.0 372.4 jit_solution(13501821842634207534)
XLA Ops:
  11.8 2.4 scatter_custom_fusion
  14.3 5.0 %gather_fusion = bf16[768]{0:T(1024)(128)(2,1)S(1)} fusion(bf16[513]{0:T(1024)(128)(2,1)S(1)} %pad_maximum_fusion, s32[1024]{0:T(1024)S(1)} %get-tuple-element.11), kind=kCustom, calls=%fused_computation | custom fusion | bytes 6144 | tf_op jit(solution)/shard_map/gather | solution.py:35
  21.3 8.2 %gather_fusion.1 = bf16[768,2048]{1,0:T(8,128)(2,1)} fusion(bf16[129,2048]{1,0:T(8,128)(2,1)} %concatenate.10, s32[1024]{0:T(1024)S(1)} %get-tuple-element.10), kind=kCustom, calls=%fused_computation.1 | custom fusion | bytes 6294528 | tf_op jit(solution)/shard_map/gather | solution.py:61
  29.5 4.2 %fusion = bf16[4,2,96,2048]{3,2,1,0:T(8,128)(2,1)} fusion(bf16[4,2,96,2048]{3,2,1,0:T(8,128)(2,1)} %bitcast.77, f32[4,2,96]{2,1,0:T(2,128)S(1)} %reshape.96), kind=kLoop, calls=%fused_computation.7 | loop fusion | flops 4718592 | bytes 6294528 | tf_op jit(solution)/shard_map/convert_element_type | solution.py:62
  33.7 4.6 %all-to-all-start = ((bf16[4,2,96,2048]{3,2,1,0:T(8,128)(2,1)}), bf16[4,2,96,2048]{3,2,1,0:T(8,128)(2,1)}, u32[]{:S(2)}, u32[]{:S(2)}) async-start(bf16[4,2,96,2048]{3,2,1,0:T(8,128)(2,1)} %fusion), calls=%async_computation | async-start | bytes 6291456 | tf_op jit(solution)/shard_map/all_to_all | solution.py:65
  40.3 8.2 %gather_fusion.2 = bf16[768,2048]{1,0:T(8,128)(2,1)} fusion(bf16[129,2048]{1,0:T(8,128)(2,1)} %concatenate.11, s32[1024]{0:T(1024)S(1)} %get-tuple-element.10), kind=kCustom, calls=%fused_computation.2 | custom fusion | bytes 6294528 | tf_op jit(solution)/shard_map/gather | solution.py:34
  48.5 27.5 %all-to-all-done = bf16[4,2,96,2048]{3,2,1,0:T(8,128)(2,1)} async-done(((bf16[4,2,96,2048]{3,2,1,0:T(8,128)(2,1)}), bf16[4,2,96,2048]{3,2,1,0:T(8,128)(2,1)}, u32[]{:S(2)}, u32[]{:S(2)}) %all-to-all-start) | async-done | bytes 3145760 | tf_op jit(solution)/shard_map/all_to_all | solution.py:65
  76.0 4.6 %all-to-all-start.1 = ((bf16[4,2,96,2048]{3,2,1,0:T(8,128)(2,1)}), bf16[4,2,96,2048]{3,2,1,0:T(8,128)(2,1)}, u32[]{:S(2)}, u32[]{:S(2)}) async-start(bf16[4,2,96,2048]{3,2,1,0:T(8,128)(2,1)} %bitcast.76), calls=%async_computation.1 | async-start | bytes 6291456 | tf_op jit(solution)/shard_map/all_to_all | solution.py:36
  80.9 5.7 %fusion.25 = f32[4,2,96,384]{3,2,0,1:T(8,128)} fusion(bf16[2,2048,384]{2,1,0:T(8,128)(2,1)} %param.13, bf16[4,2,96,2048]{3,2,1,0:T(8,128)(2,1)} %all-to-all-done), kind=kOutput, calls=%fused_computation.29 | convolution fusion | flops 1207959552 | bytes 7471104 | tf_op jit(solution)/shard_map/secd,edf->secf/dot_general | solution.py:68
  86.6 31.1 %all-to-all-done.1 = bf16[4,2,96,2048]{3,2,1,0:T(8,128)(2,1)} async-done(((bf16[4,2,96,2048]{3,2,1,0:T(8,128)(2,1)}), bf16[4,2,96,2048]{3,2,1,0:T(8,128)(2,1)}, u32[]{:S(2)}, u32[]{:S(2)}) %all-to-all-start.1) | async-done | bytes 3145760 | tf_op jit(solution)/shard_map/all_to_all | solution.py:36
  117.7 4.7 %fusion.30 = f32[4,2,96,384]{3,2,0,1:T(8,128)S(1)} fusion(bf16[2,2048,384]{2,1,0:T(8,128)(2,1)} %param.11, bf16[4,2,96,2048]{3,2,1,0:T(8,128)(2,1)} %all-to-all-done.1), kind=kOutput, calls=%fused_computation.30 | convolution fusion | flops 1207959552 | bytes 7471104 | tf_op jit(solution)/shard_map/secd,edf->secf/dot_general | solution.py:37
  122.4 5.0 %multiply_convert_fusion = (bf16[4,2,96,384]{3,2,0,1:T(8,128)(2,1)S(1)}, bf16[4,2,96,384]{3,2,0,1:T(8,128)(2,1)}, bf16[4,2,96,384]{3,2,0,1:T(8,128)(2,1)}) fusion(f32[4,2,96,384]{3,2,0,1:T(8,128)S(1)} %fusion.30, f32[4,2,96,384]{3,2,0,1:T(8,128)S(1)} %copy-done.3, bf16[2,2048,384]{2,1,0:T(8,128)(2,1)S(1)} %copy-done, ...), kind=kOutput, calls=%fused_computation.31 | convolution fusion | flops 1212678144 | bytes 10420224 | tf_op jit(solution)/shard_map/secd,edf->secf/dot_general | solution.py:40
  128.2 5.7 %bitcast_convert_fusion = bf16[2,2048,384]{2,1,0:T(8,128)(2,1)} fusion(bf16[4,2,96,2048]{3,2,1,0:T(8,128)(2,1)} %all-to-all-done, bf16[4,2,96,384]{3,2,0,1:T(8,128)(2,1)S(1)} %get-tuple-element.5), kind=kOutput, calls=%fused_computation.8 | convolution fusion | flops 1209532416 | bytes 6881280 | tf_op jit(solution)/shard_map/secd,secf->edf/dot_general | solution.py:75
  134.0 5.8 %bitcast_convert_fusion.2 = bf16[2,2048,384]{2,1,0:T(8,128)(2,1)} fusion(bf16[4,2,96,2048]{3,2,1,0:T(8,128)(2,1)} %all-to-all-done.1, bf16[4,2,96,384]{3,2,0,1:T(8,128)(2,1)} %get-tuple-element.6), kind=kOutput, calls=%fused_computation.10 | convolution fusion | flops 1209532416 | bytes 6881280 | tf_op jit(solution)/shard_map/secd,secf->edf/dot_general | solution.py:76
  139.9 5.8 %bitcast_convert_fusion.1 = bf16[2,2048,384]{2,1,0:T(8,128)(2,1)} fusion(bf16[4,2,96,2048]{3,2,1,0:T(8,128)(2,1)} %all-to-all-done.1, bf16[4,2,96,384]{3,2,0,1:T(8,128)(2,1)} %get-tuple-element.7), kind=kOutput, calls=%fused_computation.9 | convolution fusion | flops 1209532416 | bytes 6881280 | tf_op jit(solution)/shard_map/secd,secf->edf/dot_general | solution.py:79
  145.7 3.9 %fusion.15 = bf16[4,2,96,2048]{3,2,0,1:T(8,128)(2,1)S(1)} fusion(bf16[4,2,96,384]{3,2,0,1:T(8,128)(2,1)} %copy-done.2, bf16[2,2048,384]{2,1,0:T(8,128)(2,1)} %param.13), kind=kOutput, calls=%fused_computation.25 | convolution fusion | flops 1209532416 | bytes 6881280 | tf_op jit(solution)/shard_map/secf,edf->secd/dot_general | solution.py:43
  151.5 4.9 %all-to-all-start.3 = ((bf16[4,2,96,2048]{3,2,1,0:T(8,128)(2,1)}), bf16[4,2,96,2048]{3,2,1,0:T(8,128)(2,1)}, u32[]{:S(2)}, u32[]{:S(2)}) async-start(bf16[4,2,96,2048]{3,2,1,0:T(8,128)(2,1)} %copy.29), calls=%async_computation.3 | async-start | bytes 6291456 | tf_op jit(solution)/shard_map/all_to_all | solution.py:54
  156.4 4.0 %fusion.1 = f32[2,4,96,2048]{3,2,1,0:T(8,128)S(1)} fusion(bf16[4,2,96,384]{3,2,0,1:T(8,128)(2,1)} %get-tuple-element.6, bf16[2,2048,384]{2,1,0:T(8,128)(2,1)} %param.11), kind=kOutput, calls=%fused_computation.13 | convolution fusion | flops 1207959552 | bytes 10027008 | tf_op jit(solution)/shard_map/secf,edf->secd/dot_general | solution.py:81
  162.3 2.0 copy.28
  164.4 29.0 %all-to-all-done.3 = bf16[4,2,96,2048]{3,2,1,0:T(8,128)(2,1)} async-done(((bf16[4,2,96,2048]{3,2,1,0:T(8,128)(2,1)}), bf16[4,2,96,2048]{3,2,1,0:T(8,128)(2,1)}, u32[]{:S(2)}, u32[]{:S(2)}) %all-to-all-start.3) | async-done | bytes 3145760 | tf_op jit(solution)/shard_map/all_to_all | solution.py:54
  193.4 4.6 %all-to-all-start.2 = ((bf16[4,2,96,2048]{3,2,1,0:T(8,128)(2,1)}), bf16[4,2,96,2048]{3,2,1,0:T(8,128)(2,1)}, u32[]{:S(2)}, u32[]{:S(2)}) async-start(bf16[4,2,96,2048]{3,2,1,0:T(8,128)(2,1)} %copy.28), calls=%async_computation.2 | async-start | bytes 6291456 | tf_op jit(solution)/shard_map/all_to_all | solution.py:84
  198.1 7.6 %gather_fusion.4 = bf16[512,2048]{1,0:T(8,128)(2,1)} fusion(bf16[768,2048]{1,0:T(8,128)(2,1)} %bitcast.20, s32[1024]{0:T(1024)S(1)} %pad_clamp_fusion), kind=kCustom, calls=%fused_computation.4 | custom fusion | bytes 4196352 | tf_op jit(solution)/shard_map/gather | solution.py:55
  205.6 4.1 %reshape.95 = bf16[128,4,2048]{2,1,0:T(4,128)(2,1)} reshape(bf16[512,2048]{1,0:T(8,128)(2,1)} %gather_fusion.4) | data formatting | bytes 4194304 | tf_op jit(solution)/shard_map/reshape | solution.py:55
  209.8 4.5 %fusion.35 = bf16[128,1,4]{2,1,0:T(2,128)(2,1)S(1)} fusion(bf16[128,4,2048]{2,1,0:T(4,128)(2,1)} %reshape.95, bf16[128,2048,1]{1,0,2:T(8,128)(2,1)} %bitcast.78), kind=kOutput, calls=%fused_computation.35 | convolution fusion | flops 2097152 | bytes 2622464 | tf_op jit(solution)/shard_map/tkd,td->tk/dot_general | solution.py:58
  214.9 20.2 %all-to-all-done.2 = bf16[4,2,96,2048]{3,2,1,0:T(8,128)(2,1)} async-done(((bf16[4,2,96,2048]{3,2,1,0:T(8,128)(2,1)}), bf16[4,2,96,2048]{3,2,1,0:T(8,128)(2,1)}, u32[]{:S(2)}, u32[]{:S(2)}) %all-to-all-start.2) | async-done | bytes 3145760 | tf_op jit(solution)/shard_map/all_to_all | solution.py:84
  235.1 7.6 %gather_fusion.3 = bf16[512,2048]{1,0:T(8,128)(2,1)} fusion(bf16[768,2048]{1,0:T(8,128)(2,1)} %bitcast.17, s32[1024]{0:T(1024)S(1)} %pad_clamp_fusion), kind=kCustom, calls=%fused_computation.3 | custom fusion | bytes 4196352 | tf_op jit(solution)/shard_map/gather | solution.py:85
  242.7 4.1 %reshape.93 = bf16[128,4,2048]{2,1,0:T(4,128)(2,1)} reshape(bf16[512,2048]{1,0:T(8,128)(2,1)} %gather_fusion.3) | data formatting | bytes 4194304 | tf_op jit(solution)/shard_map/reshape | solution.py:85
  246.8 5.0 %reduce_sum.25 = bf16[128,2048]{1,0:T(8,128)(2,1)} reduce(bf16[128,4,2048]{2,1,0:T(4,128)(2,1)} %reshape.93, bf16[]{:T(256)} %constant.34.clone.1), dimensions={1}, to_apply=%region_4.5 | reduce | flops 786432 | bytes 2621442 | tf_op jit(solution)/shard_map/reduce_sum | solution.py:88
  251.9 1.9 convert_element_type.92
  253.8 33.1 %reduce-scatter.4.cloned.1.call-done = bf16[2,256,384]{2,1,0:T(8,128)(2,1)} async-done(((bf16[2,2048,384]{2,1,0:T(8,128)(2,1)}), bf16[2,256,384]{2,1,0:T(8,128)(2,1)}) %reduce-scatter.4.cloned.1.call-update) | async-done | bytes 393232 | tf_op jit(solution)/shard_map/reduce_scatter | solution.py:90
  286.9 1.9 convert_element_type.88
  288.8 75.2 %reduce-scatter.6.cloned.1.call-done = bf16[2,256,384]{2,1,0:T(8,128)(2,1)} async-done(((bf16[2,2048,384]{2,1,0:T(8,128)(2,1)}), bf16[2,256,384]{2,1,0:T(8,128)(2,1)}) %reduce-scatter.6.cloned.1.call-update) | async-done | bytes 393232 | tf_op jit(solution)/shard_map/reduce_scatter | solution.py:93
  (42 shorter events, 16.0 us)
Async XLA Ops:
  7.2 115.2 %copy-start = (bf16[2,2048,384]{2,1,0:T(8,128)(2,1)S(1)}, bf16[2,2048,384]{2,1,0:T(8,128)(2,1)}, u32[]{:S(2)}) copy-start(bf16[2,2048,384]{2,1,0:T(8,128)(2,1)} %param.12) | copy-start | bytes 9437188
  33.7 42.3 %all-to-all-start = ((bf16[4,2,96,2048]{3,2,1,0:T(8,128)(2,1)}), bf16[4,2,96,2048]{3,2,1,0:T(8,128)(2,1)}, u32[]{:S(2)}, u32[]{:S(2)}) async-start(bf16[4,2,96,2048]{3,2,1,0:T(8,128)(2,1)} %fusion), calls=%async_computation | async-start | bytes 6291456 | tf_op jit(solution)/shard_map/all_to_all | solution.py:65
  76.0 41.6 %all-to-all-start.1 = ((bf16[4,2,96,2048]{3,2,1,0:T(8,128)(2,1)}), bf16[4,2,96,2048]{3,2,1,0:T(8,128)(2,1)}, u32[]{:S(2)}, u32[]{:S(2)}) async-start(bf16[4,2,96,2048]{3,2,1,0:T(8,128)(2,1)} %bitcast.76), calls=%async_computation.1 | async-start | bytes 6291456 | tf_op jit(solution)/shard_map/all_to_all | solution.py:36
  80.7 171.2 %reduce-scatter.8.cloned.1.call-start = ((), (), s32[]{:S(2)}) async-start(), calls=%async_computation.9 | async-start | bytes 3538944 | tf_op jit(solution)/shard_map/reduce_scatter | solution.py:96
  117.7 4.7 %copy-start.3 = (f32[4,2,96,384]{3,2,0,1:T(8,128)S(1)}, f32[4,2,96,384]{3,2,0,1:T(8,128)}, u32[]{:S(2)}) copy-start(f32[4,2,96,384]{3,2,0,1:T(8,128)} %fusion.25) | copy-start | bytes 3538948
  127.4 0.8 copy-start.2
  133.9 152.9 %reduce-scatter.4.cloned.1.call-start = ((), (), s32[]{:S(2)}) async-start(), calls=%async_computation.7 | async-start | bytes 3538944 | tf_op jit(solution)/shard_map/reduce_scatter | solution.py:90
  139.8 224.1 %reduce-scatter.6.cloned.1.call-start = ((), (), s32[]{:S(2)}) async-start(), calls=%async_computation.8 | async-start | bytes 3538944 | tf_op jit(solution)/shard_map/reduce_scatter | solution.py:93
  151.5 41.9 %all-to-all-start.3 = ((bf16[4,2,96,2048]{3,2,1,0:T(8,128)(2,1)}), bf16[4,2,96,2048]{3,2,1,0:T(8,128)(2,1)}, u32[]{:S(2)}, u32[]{:S(2)}) async-start(bf16[4,2,96,2048]{3,2,1,0:T(8,128)(2,1)} %copy.29), calls=%async_computation.3 | async-start | bytes 6291456 | tf_op jit(solution)/shard_map/all_to_all | solution.py:54
  156.4 4.0 %copy-start.1 = (bf16[4,2,96,384]{3,2,0,1:T(8,128)(2,1)S(1)}, bf16[4,2,96,384]{3,2,0,1:T(8,128)(2,1)}, u32[]{:S(2)}) copy-start(bf16[4,2,96,384]{3,2,0,1:T(8,128)(2,1)} %get-tuple-element.7) | copy-start | bytes 1769476
  193.4 41.6 %all-to-all-start.2 = ((bf16[4,2,96,2048]{3,2,1,0:T(8,128)(2,1)}), bf16[4,2,96,2048]{3,2,1,0:T(8,128)(2,1)}, u32[]{:S(2)}, u32[]{:S(2)}) async-start(bf16[4,2,96,2048]{3,2,1,0:T(8,128)(2,1)} %copy.28), calls=%async_computation.2 | async-start | bytes 6291456 | tf_op jit(solution)/shard_map/all_to_all | solution.py:84
Sparse Core Ops, SparseCore 0:
  134.1 75.5 reduce-scatter.7
  213.2 73.6 reduce-scatter.3
  290.4 73.4 reduce-scatter.5
where the time goes:
time: 374 us; the launch traced here: 372 us
  waiting for transfers between devices  216 us (58%)
  local copies, waits for them, and re-layouts  59.1 us (16%)
  matrix products  47 us (13%)
  starting transfers between devices  19.1 us (5%)
  other arithmetic  17.1 us (5%)
  between operations  13.9 us (4%)
    reduce_scatter x1, waiting for transfers between devices, local(): lax.psum_scatter(up_terms.astype(jnp.bfloat16), 'dp', scatter_dimension=1...  75.2 us
    reduce_scatter x1, waiting for transfers between devices, local(): lax.psum_scatter(gate_terms.astype(jnp.bfloat16), 'dp', scatter_dimension...  33.1 us
    all_to_all x1, waiting for transfers between devices, local(): lax.all_to_all(sent_rows, 'expert', split_axis=0, concat_axis=0, tiled=True)  31.1 us
    all_to_all x1, waiting for transfers between devices, local(): lax.all_to_all(expert_out, 'expert', split_axis=0, concat_axis=0, tiled=T...  29 us
    all_to_all x1, waiting for transfers between devices, local(): lax.all_to_all(weighted.reshape(layout + (model_width,)), 'expert', split...  27.5 us
    all_to_all x1, waiting for transfers between devices, local(): lax.all_to_all(rows_cot, 'expert', split_axis=0, concat_axis=0, tiled=True)  20.2 us
    gather x1, local copies, waits for them, and re-layouts, local(): cot_rows = cot_pad[source_rows]  8.23 us
    gather x1, local copies, waits for them, and re-layouts, local(): sent_rows = token_pad[source_rows].reshape(layout + (model_width,))  8.23 us
  transfers between devices with their start and end apart: 7, of which 6 were waited for; matrix products, arithmetic and copies ran while one was open for 21% of the time, Pallas kernels for 0%

commit v1 on v0

v1 whole, which is shorter than its diff:
```python
import functools

import jax
import jax.numpy as jnp
from jax import lax
from jax.experimental import pallas as pl
from jax.experimental.pallas import tpu as pltpu
from jax.sharding import PartitionSpec as P

MESH = pl.DeviceIdType.MESH
LANES = 128
PARTS = 2


def bit_of(index, bit):
    return (index // (1 << bit)) % 2


def flipped(index, bit):
    return index + (1 << bit) * (1 - 2 * bit_of(index, bit))


def partner_mask(index, mask, bits):
    for bit in range(bits):
        if mask >> bit & 1:
            index = flipped(index, bit)
    return index


def position(owner, order):
    place = 0
    for bit in order:
        place = place * 2 + bit_of(owner, bit)
    return place


class Halving:
    def __init__(self, axis, order, buf, recv, send_sem, recv_sem):
        self.axis, self.order, self.buf, self.recv = axis, order, buf, recv
        self.send_sem, self.recv_sem = send_sem, recv_sem
        self.me = lax.axis_index(axis)
        self.count = 1 << len(order)
        self.copies = []

    def base(self, stage):
        place = 0
        for step in range(stage):
            place = place + bit_of(self.me, self.order[step]) * (self.count >> (step + 1))
        return place

    def start(self, stage):
        size = self.count >> (stage + 1)
        bit = self.order[stage]
        begin = self.base(stage) + (1 - bit_of(self.me, bit)) * size
        offset = self.count - (self.count >> stage)
        copy = pltpu.make_async_remote_copy(
            src_ref=self.buf.at[pl.ds(begin, size)],
            dst_ref=self.recv.at[pl.ds(offset, size)],
            send_sem=self.send_sem.at[stage],
            recv_sem=self.recv_sem.at[stage],
            device_id={self.axis: flipped(self.me, bit)},
            device_id_type=MESH,
        )
        copy.start()
        self.copies.append(copy)

    def received(self, stage):
        self.copies[stage].wait_recv()
        size = self.count >> (stage + 1)
        begin = self.base(stage + 1)
        offset = self.count - (self.count >> stage)
        kept = self.buf[pl.ds(begin, size)].astype(jnp.float32)
        return begin, size, kept + self.recv[pl.ds(offset, size)].astype(jnp.float32)

    def step(self, stage):
        begin, size, total = self.received(stage)
        if stage == len(self.order) - 1:
            return total[0]
        self.buf[pl.ds(begin, size)] = total.astype(jnp.bfloat16)
        self.start(stage + 1)
        return None

    def finish(self):
        for copy in self.copies:
            copy.wait_send()


def contract(left, right, dims):
    return lax.dot_general(left, right, (dims, ((), ())), preferred_element_type=jnp.float32)


def kernel(
    ranks, groups,
    tok_hbm, cot_hbm, wd_hbm, gate_hbm, up_hbm, down_hbm,
    tok_out, score_out, gate_out, up_out, down_out,
    x_buf, c_buf, w_buf, weights, cots, parts, parts_recv, score, score_recv,
    local_sem, gather_send, gather_recv, part_send, part_recv,
    tok_send, tok_recv, score_send, score_recv_sem, ready,
):
    rank_bits, group_bits = ranks.bit_length() - 1, groups.bit_length() - 1
    me, group = lax.axis_index("expert"), lax.axis_index("dp")
    experts_here, width, hidden_units = weights.shape[1:]
    rows = x_buf.shape[1]
    owned = width // groups
    part_rows = owned // PARTS

    loads = [
        pltpu.make_async_copy(src, weights.at[i], local_sem.at[i])
        for i, src in enumerate((gate_hbm, up_hbm, down_hbm))
    ]
    own = [
        pltpu.make_async_copy(src, dst.at[me], local_sem.at[3 + i])
        for i, (src, dst) in enumerate(((tok_hbm, x_buf), (cot_hbm, c_buf), (wd_hbm, w_buf)))
    ]
    for copy in own + loads:
        copy.start()

    barrier = pltpu.get_barrier_semaphore()
    for bit in range(rank_bits):
        pl.semaphore_signal(barrier, 1, device_id={"expert": flipped(me, bit)}, device_id_type=MESH)
    for bit in range(group_bits):
        pl.semaphore_signal(barrier, 1, device_id={"dp": flipped(group, bit)}, device_id_type=MESH)
    pl.semaphore_wait(barrier, rank_bits + group_bits)

    gathered = {}

    def send_block(mask, bit, i):
        block = partner_mask(me, mask, rank_bits)
        dst = (x_buf, c_buf, w_buf)[i]
        slot = mask | 1 << bit
        copy = pltpu.make_async_remote_copy(
            src_ref=(tok_hbm, cot_hbm, wd_hbm)[i] if mask == 0 else dst.at[block],
            dst_ref=dst.at[block],
            send_sem=gather_send.at[slot, i],
            recv_sem=gather_recv.at[slot, i],
            device_id={"expert": flipped(me, bit)},
            device_id_type=MESH,
        )
        copy.start()
        gathered[slot, i] = copy

    for i in (2, 0, 1):
        for bit in reversed(range(rank_bits)):
            send_block(0, bit, i)

    lane = lax.broadcasted_iota(jnp.int32, (rows, LANES), 1)

    def forward(block):
        x, c = x_buf[block], c_buf[block]
        route_weights = w_buf[block].astype(jnp.float32)
        scores = jnp.zeros((rows, LANES), jnp.float32)
        for e in range(experts_here):
            mine = lane == me * experts_here + e
            weight = jnp.sum(jnp.where(mine, route_weights, 0.0), axis=1, keepdims=True)
            gate = contract(x, weights[0, e], ((1,), (0,)))
            up = contract(x, weights[1, e], ((1,), (0,)))
            back = contract(c, weights[2, e], ((1,), (0,)))
            sig = jax.nn.sigmoid(gate)
            act = gate * sig
            hidden = (act * up).astype(jnp.bfloat16).astype(jnp.float32)
            scores = jnp.where(mine, jnp.sum(back * hidden, axis=1, keepdims=True), scores)
            back = back * weight
            gate_cot = back * up * sig * (1.0 + gate * (1.0 - sig))
            for kind, value in enumerate((gate_cot, back * act, hidden * weight)):
                at = (kind * experts_here + e) * hidden_units
                cots[block, :, at:at + hidden_units] = value.astype(jnp.bfloat16)
        score[position(block, range(rank_bits))] = scores.astype(jnp.bfloat16)

    for copy in own + loads:
        copy.wait()
    forward(me)
    for mask in range(1, ranks):
        lowest = (mask & -mask).bit_length() - 1
        for i in (2, 0, 1):
            gathered[mask, i].wait_recv()
            for bit in reversed(range(lowest)):
                send_block(mask, bit, i)
        forward(partner_mask(me, mask, rank_bits))
    for copy in gathered.values():
        copy.wait_send()

    first = list(range(group_bits))
    second = [1, 0] + first[2:] if group_bits > 1 else first
    chunks = []

    def weight_grads(kind, source):
        at = kind * experts_here * hidden_units
        orders = [[second if e == 0 and q == 0 else first for q in range(PARTS)]
                  for e in range(experts_here)]

        def one(owner, _):
            columns = pl.ds(pl.multiple_of(owner * owned, LANES), owned)
            left = source[:, :, columns].reshape(ranks * rows, owned)
            right = cots[:, :, at:at + experts_here * hidden_units]
            right = right.reshape(ranks * rows, experts_here * hidden_units)
            total = contract(left, right, ((0,), (0,))).astype(jnp.bfloat16)
            for e in range(experts_here):
                for q in range(PARTS):
                    parts[kind, e, q, position(owner, orders[e][q])] = total[
                        q * part_rows:(q + 1) * part_rows, e * hidden_units:(e + 1) * hidden_units
                    ]
            return 0

        lax.fori_loop(0, groups, one, 0)
        for e in range(experts_here):
            for q in range(PARTS):
                job = Halving(
                    "dp", orders[e][q], parts.at[kind, e, q], parts_recv.at[kind, e, q],
                    part_send.at[kind, e, q], part_recv.at[kind, e, q],
                )
                job.start(0)
                chunks.append((job, kind, e, q))

    weight_grads(2, c_buf)
    for bit in range(rank_bits):
        pl.semaphore_signal(
            ready.at[bit], 1, device_id={"expert": flipped(me, bit)}, device_id_type=MESH
        )
    weight_grads(0, x_buf)
    weight_grads(1, x_buf)

    def token_part(step, _):
        strip = 2 * LANES
        columns = pl.ds(pl.multiple_of(step * strip, LANES), strip)
        total = jnp.zeros((ranks * rows, strip), jnp.float32)
        for kind in range(2):
            for e in range(experts_here):
                at = (kind * experts_here + e) * hidden_units
                left = cots[:, :, at:at + hidden_units].reshape(ranks * rows, hidden_units)
                total += contract(left, weights[kind, e, columns, :], ((1,), (1,)))
        total = total.astype(jnp.bfloat16)
        for r in range(ranks):
            x_buf[position(r, range(rank_bits)), :, columns] = total[r * rows:(r + 1) * rows]
        return 0

    lax.fori_loop(0, width // (2 * LANES), token_part, 0)
    order = list(range(rank_bits))
    token_job = Halving("expert", order, x_buf, c_buf, tok_send, tok_recv)
    score_job = Halving("expert", order, score, score_recv, score_send, score_recv_sem)
    for bit in range(rank_bits):
        pl.semaphore_wait(ready.at[bit], 1)
    token_job.start(0)
    score_job.start(0)

    outs = (gate_out, up_out, down_out)
    for turn in range(len(chunks) + group_bits - 1):
        for stage in range(group_bits):
            if 0 <= turn - stage < len(chunks):
                job, kind, e, q = chunks[turn - stage]
                total = job.step(stage)
                if total is not None:
                    outs[kind][e, q * part_rows:(q + 1) * part_rows, :] = total
        if turn < rank_bits:
            total = token_job.step(turn)
            if total is not None:
                tok_out[...] = total.astype(jnp.bfloat16)
            total = score_job.step(turn)
            if total is not None:
                score_out[...] = total.astype(jnp.bfloat16)
    for job in [chunk[0] for chunk in chunks] + [token_job, score_job]:
        job.finish()


def local(ranks, groups, tokens, routes, combine, out_cotangent, gate_weight, up_weight, down_weight):
    rows, width = tokens.shape
    experts_here, _, hidden_units = gate_weight.shape
    owned = width // groups
    lane = jnp.arange(LANES, dtype=jnp.int32)
    named = routes[:, :, None] == lane
    dense = jnp.sum(jnp.where(named, combine[:, :, None].astype(jnp.float32), 0.0), axis=1)
    dense = dense.astype(jnp.bfloat16)
    rank_bits, group_bits = ranks.bit_length() - 1, groups.bit_length() - 1
    bf16, dma = jnp.bfloat16, pltpu.SemaphoreType.DMA
    anywhere = pl.BlockSpec(memory_space=pl.ANY)
    vmem = pl.BlockSpec(memory_space=pltpu.VMEM)
    grad = jax.ShapeDtypeStruct((experts_here, owned, hidden_units), jnp.float32)
    chunk = (3, experts_here, PARTS)
    block = (owned // PARTS, hidden_units)
    token_grads, scores, gate_grads, up_grads, down_grads = pl.pallas_call(
        functools.partial(kernel, ranks, groups),
        out_shape=(
            jax.ShapeDtypeStruct((rows, width), bf16),
            jax.ShapeDtypeStruct((rows, LANES), bf16),
            grad, grad, grad,
        ),
        in_specs=[anywhere] * 6,
        out_specs=(vmem,) * 5,
        scratch_shapes=[
            pltpu.VMEM((ranks, rows, width), bf16),
            pltpu.VMEM((ranks, rows, width), bf16),
            pltpu.VMEM((ranks, rows, LANES), bf16),
            pltpu.VMEM((3,) + gate_weight.shape, bf16),
            pltpu.VMEM((ranks, rows, 3 * experts_here * hidden_units), bf16),
            pltpu.VMEM(chunk + (groups,) + block, bf16),
            pltpu.VMEM(chunk + (groups - 1,) + block, bf16),
            pltpu.VMEM((ranks, rows, LANES), bf16),
            pltpu.VMEM((ranks, rows, LANES), bf16),
            dma((6,)),
            dma((ranks, 3)),
            dma((ranks, 3)),
            dma(chunk + (group_bits,)),
            dma(chunk + (group_bits,)),
            dma((rank_bits,)),
            dma((rank_bits,)),
            dma((rank_bits,)),
            dma((rank_bits,)),
            pltpu.SemaphoreType.REGULAR((rank_bits,)),
        ],
        compiler_params=pltpu.CompilerParams(
            collective_id=0, has_side_effects=True, vmem_limit_bytes=62 * 2**20
        ),
    )(tokens, out_cotangent, dense, gate_weight, up_weight, down_weight)
    picked = jnp.where(named, scores[:, None, :].astype(jnp.float32), 0.0)
    combine_grads = jnp.sum(picked, axis=2).astype(bf16)
    return token_grads, combine_grads, gate_grads, up_grads, down_grads


def solution(mesh):
    ranks, groups = mesh.shape["expert"], mesh.shape["dp"]
    return jax.shard_map(
        functools.partial(local, ranks, groups),
        mesh=mesh,
        in_specs=(
            P(("dp", "expert"), None),
            P(("dp", "expert"), None),
            P(("dp", "expert"), None),
            P(("dp", "expert"), None),
            P("expert", None, None),
            P("expert", None, None),
            P("expert", None, None),
        ),
        out_specs=(
            P(("dp", "expert"), None),
            P(("dp", "expert"), None),
            P("expert", "dp", None),
            P("expert", "dp", None),
            P("expert", "dp", None),
        ),
        check_vma=False,
    )
```

time: 374 us -> 196 us (0.52)
  waiting for transfers between devices: 216 us -> 0 us
  Pallas kernels: 0 us -> 186 us
  local copies, waits for them, and re-layouts: 59.1 us -> 5.71 us
  matrix products: 47 us -> 0 us
  starting transfers between devices: 19.1 us -> 0 us
  between operations: 13.9 us -> 0.66 us
  other arithmetic: 17.1 us -> 3.88 us
    pallas_call x0 -> x1, Pallas kernels: none -> 186 us  [local(): pl.pallas_call(functools.partial(kernel, ranks, groups), out_shape=(jax.S...]
    reduce_scatter x3 -> x0, waiting for transfers between devices: 108 us -> none  [the longest x1 75.2 us: local(): lax.psum_scatter(up_terms.astype(jnp.bfloat16), 'dp', scatter_dimension=1...]
    all_to_all x4 -> x0, waiting for transfers between devices: 108 us -> none  [the longest x1 31.1 us: local(): lax.all_to_all(sent_rows, 'expert', split_axis=0, concat_axis=0, tiled=True)]
    dot_general x10 -> x0, matrix products: 47 us -> none  [the longest x1 5.83 us: local(): jnp.einsum('secd,secf->edf', token_rows, gate_cot, preferred_element_type...]
    gather x5 -> x0, local copies, waits for them, and re-layouts: 36.7 us -> none  [the longest x1 8.23 us: local(): cot_rows = cot_pad[source_rows]]
    all_to_all x4 -> x0, starting transfers between devices: 18.8 us -> none  [the longest x1 4.9 us: local(): lax.all_to_all(expert_out, 'expert', split_axis=0, concat_axis=0, tiled=T...]
    convert_element_type x5 -> x2, other arithmetic: 9.94 us -> 1.56 us  [the longest x1 0.88 us: local(): picked = jnp.where(named, scores[:, None, :].astype(jnp.float32), 0.0)]
    reshape x3 -> x0, local copies, waits for them, and re-layouts: 8.35 us -> none  [the longest x1 4.12 us: local(): dgrad_rows.reshape(experts * capacity, model_width)[slot_ids]]
  transfers between devices with their start and end apart: 7 -> 0, of which waited for: 6 -> 0; matrix products, arithmetic and copies ran while one was open for 21% -> 0% of each run, Pallas kernels for 0% -> 0%
where the time goes in v1:
time: 196 us
  Pallas kernels  186 us (95%)
  local copies, waits for them, and re-layouts  5.71 us (3%)
  other arithmetic  3.88 us (2%)
    pallas_call x1, Pallas kernels, local(): pl.pallas_call(functools.partial(kernel, ranks, groups), out_shape=(jax.S...  186 us
    unnamed x10, local copies, waits for them, and re-layouts  5.71 us

profile of v1, /device:TPU:0, one launch (start us, length us, event | category | flops | bytes accessed | tf_op | source)
XLA Modules:
  0.0 196.0 jit_solution(8732264215078017888)
XLA Ops:
  0.6 0.7 convert_element_type.14
  1.3 1.5 select_reduce_fusion.1.wd_hbm
  2.8 0.0 copy-start.2
  2.8 185.8 %shard_map.110 = (bf16[128,2048]{1,0:T(8,128)(2,1)}, bf16[128,128]{1,0:T(8,128)(2,1)}, f32[2,256,384]{2,1,0:T(8,128)}, f32[2,256,384]{2,1,0:T(8,128)}, f32[2,256,384]{2,1,0:T(8,128)}) custom-call(bf16[128,2048]{1,0:T(8,128)(2,1)} %tok_hbm.1, bf16[128,2048]{1,0:T(8,128)(2,1)} %cot_hbm.1, bf16[128,128]{1,0:T(8,128)(2,1)} %select_reduce_fusion.1.wd_hbm, ...), custom_call_target="tpu_custom_call" | custom-call | tf_op jit(solution)/shard_map/pallas_call | solution.py:279
  188.6 0.0 copy-start.1
  188.6 0.0 copy-start
  188.6 0.9 convert_element_type.16
  189.5 0.0 copy-done.2
  189.5 0.8 select_reduce_fusion
  190.3 1.9 copy.18
  192.2 2.1 %copy.19 = f32[2,256,384]{2,1,0:T(8,128)} copy(f32[2,256,384]{2,1,0:T(8,128)} %get-tuple-element.22) | data formatting | bytes 1572864
  194.2 0.0 copy-done.1
  194.2 0.9 copy.20
  195.1 0.0 copy-done
  195.1 0.9 copy.21
Async XLA Ops:
  2.8 186.7 %copy-start.2 = (s32[128,4]{0,1:T(4,128)S(1)}, s32[128,4]{0,1:T(4,128)}, u32[]{:S(2)}) copy-start(s32[128,4]{0,1:T(4,128)} %param.8) | copy-start | bytes 6148
  188.6 5.7 %copy-start.1 = (f32[2,256,384]{2,1,0:T(8,128)S(1)}, f32[2,256,384]{2,1,0:T(8,128)}, u32[]{:S(2)}) copy-start(f32[2,256,384]{2,1,0:T(8,128)} %get-tuple-element.23) | copy-start | bytes 2359300
  188.6 6.5 %copy-start = (f32[2,256,384]{2,1,0:T(8,128)S(1)}, f32[2,256,384]{2,1,0:T(8,128)}, u32[]{:S(2)}) copy-start(f32[2,256,384]{2,1,0:T(8,128)} %get-tuple-element.24) | copy-start | bytes 2359300

commit v2 on v1

--- a/solution.py
+++ b/solution.py
@@ -85,15 +85,43 @@
             copy.wait_send()
 
 
+def plan(orders, blocks, links, depth):
+    bits = len(orders[0])
+    first_link = [links[order[0]] for order in orders]
+    free = {link: 0.0 for link in links}
+    waiting = {link: [j for j, at in enumerate(first_link) if at == link] for link in links}
+    began = {link: [] for link in links}
+    ready = []
+    events = []
+    while ready or any(waiting.values()):
+        choices = [(max(free[links[orders[j][s]]], t), 0, t, j, s) for t, j, s in ready]
+        choices += [(free[link], 1, 0.0, jobs[0], 0) for link, jobs in waiting.items() if jobs]
+        begin, fresh, at, j, s = min(choices)
+        link = links[orders[j][s]]
+        end = begin + (blocks >> (s + 1))
+        free[link] = end
+        if fresh:
+            waiting[link].pop(0)
+            began[link].append(begin)
+            back = len(began[link]) - depth
+            events.append((began[link][back] if back >= 0 else -1.0, 0, j, 0))
+        else:
+            ready.remove((at, j, s))
+        events.append((end, 1, j, s))
+        if s + 1 < bits:
+            ready.append((end, j, s + 1))
+    return [event[1:] for event in sorted(events)]
+
+
 def contract(left, right, dims):
     return lax.dot_general(left, right, (dims, ((), ())), preferred_element_type=jnp.float32)
 
 
 def kernel(
     ranks, groups,
-    tok_hbm, cot_hbm, wd_hbm, gate_hbm, up_hbm, down_hbm,
+    routes_ref, combine_ref, tok_hbm, cot_hbm, gate_hbm, up_hbm, down_hbm,
     tok_out, score_out, gate_out, up_out, down_out,
-    x_buf, c_buf, w_buf, weights, cots, parts, parts_recv, score, score_recv,
+    x_buf, c_buf, w_buf, acts, weights, cots, parts, parts_recv, score, score_recv,
     local_sem, gather_send, gather_recv, part_send, part_recv,
     tok_send, tok_recv, score_send, score_recv_sem, ready,
 ):
@@ -110,10 +138,18 @@
     ]
     own = [
         pltpu.make_async_copy(src, dst.at[me], local_sem.at[3 + i])
-        for i, (src, dst) in enumerate(((tok_hbm, x_buf), (cot_hbm, c_buf), (wd_hbm, w_buf)))
+        for i, (src, dst) in enumerate(((tok_hbm, x_buf), (cot_hbm, c_buf)))
     ]
     for copy in own + loads:
         copy.start()
+
+    top = routes_ref.shape[0]
+    expert = lax.broadcasted_iota(jnp.int32, (LANES, rows), 0)
+    named = [expert == routes_ref[k:k + 1, :] for k in range(top)]
+    dense = jnp.zeros((LANES, rows), jnp.float32)
+    for k in range(top):
+        dense = jnp.where(named[k], combine_ref[k:k + 1, :].astype(jnp.float32), dense)
+    w_buf[me] = dense.T.astype(jnp.bfloat16)
 
     barrier = pltpu.get_barrier_semaphore()
     for bit in range(rank_bits):
@@ -129,7 +165,7 @@
         dst = (x_buf, c_buf, w_buf)[i]
         slot = mask | 1 << bit
         copy = pltpu.make_async_remote_copy(
-            src_ref=(tok_hbm, cot_hbm, wd_hbm)[i] if mask == 0 else dst.at[block],
+            src_ref=(tok_hbm, cot_hbm)[i] if mask == 0 and i < 2 else dst.at[block],
             dst_ref=dst.at[block],
             send_sem=gather_send.at[slot, i],
             recv_sem=gather_recv.at[slot, i],
@@ -139,22 +175,30 @@
         copy.start()
         gathered[slot, i] = copy
 
-    for i in (2, 0, 1):
-        for bit in reversed(range(rank_bits)):
-            send_block(0, bit, i)
-
-    lane = lax.broadcasted_iota(jnp.int32, (rows, LANES), 1)
-
-    def forward(block):
-        x, c = x_buf[block], c_buf[block]
-        route_weights = w_buf[block].astype(jnp.float32)
-        scores = jnp.zeros((rows, LANES), jnp.float32)
+    for bit in reversed(range(rank_bits)):
+        send_block(0, bit, 2)
+    for bit in reversed(range(rank_bits)):
+        send_block(0, bit, 0)
+    send_block(0, 0, 1)
+
+    both = 2 * rows
+    lane = lax.broadcasted_iota(jnp.int32, (both, LANES), 1)
+
+    def forward(pair):
+        x = x_buf[pl.ds(pair, 2)].reshape(both, width)
+        for kind in range(2):
+            for e in range(experts_here):
+                acts[kind, e] = contract(x, weights[kind, e], ((1,), (0,)))
+
+    def backward(pair):
+        c = c_buf[pl.ds(pair, 2)].reshape(both, width)
+        route_weights = w_buf[pl.ds(pair, 2)].reshape(both, LANES).astype(jnp.float32)
+        scores = jnp.zeros((both, LANES), jnp.float32)
         for e in range(experts_here):
             mine = lane == me * experts_here + e
             weight = jnp.sum(jnp.where(mine, route_weights, 0.0), axis=1, keepdims=True)
-            gate = contract(x, weights[0, e], ((1,), (0,)))
-            up = contract(x, weights[1, e], ((1,), (0,)))
             back = contract(c, weights[2, e], ((1,), (0,)))
+            gate, up = acts[0, e], acts[1, e]
             sig = jax.nn.sigmoid(gate)
             act = gate * sig
             hidden = (act * up).astype(jnp.bfloat16).astype(jnp.float32)
@@ -163,30 +207,66 @@
             gate_cot = back * up * sig * (1.0 + gate * (1.0 - sig))
             for kind, value in enumerate((gate_cot, back * act, hidden * weight)):
                 at = (kind * experts_here + e) * hidden_units
-                cots[block, :, at:at + hidden_units] = value.astype(jnp.bfloat16)
-        score[position(block, range(rank_bits))] = scores.astype(jnp.bfloat16)
-
-    for copy in own + loads:
-        copy.wait()
-    forward(me)
-    for mask in range(1, ranks):
+                value = value.astype(jnp.bfloat16).reshape(2, rows, hidden_units)
+                cots[pl.ds(pair, 2), :, at:at + hidden_units] = value
+        scores = scores.astype(jnp.bfloat16)
+        for i in range(2):
+            place = position(pair + i, range(rank_bits))
+            score[place] = scores[i * rows:(i + 1) * rows]
+
+    def arrived(mask, i):
+        gathered[mask, i].wait_recv()
         lowest = (mask & -mask).bit_length() - 1
-        for i in (2, 0, 1):
-            gathered[mask, i].wait_recv()
-            for bit in reversed(range(lowest)):
-                send_block(mask, bit, i)
-        forward(partner_mask(me, mask, rank_bits))
-    for copy in gathered.values():
-        copy.wait_send()
+        for bit in reversed(range(lowest)):
+            send_block(mask, bit, i)
+
+    own_pair = me // 2 * 2
+    own[0].wait()
+    loads[0].wait()
+    loads[1].wait()
+    arrived(1, 0)
+    forward(own_pair)
+    own[1].wait()
+    loads[2].wait()
+    arrived(1, 1)
+    arrived(1, 2)
+    backward(own_pair)
+    for bit in reversed(range(1, rank_bits)):
+        gathered[1 << bit, 0].wait_send()
+        send_block(0, bit, 1)
+    for mask in range(2, ranks, 2):
+        pair = partner_mask(own_pair, mask, rank_bits)
+        for i in (2, 0):
+            arrived(mask, i)
+            arrived(mask + 1, i)
+        forward(pair)
+        arrived(mask, 1)
+        arrived(mask + 1, 1)
+        backward(pair)
+    early = [(1 << bit, 0) for bit in range(1, rank_bits)]
+    for key, copy in gathered.items():
+        if key not in early:
+            copy.wait_send()
 
     first = list(range(group_bits))
     second = [1, 0] + first[2:] if group_bits > 1 else first
+    second_at = [(e, q) for e in range(experts_here) for q in range(PARTS)][:1]
     chunks = []
+    for kind in (2, 0, 1):
+        for e in range(experts_here):
+            for q in range(PARTS):
+                job = Halving(
+                    "dp", second if (e, q) in second_at else first,
+                    parts.at[kind, e, q], parts_recv.at[kind, e, q],
+                    part_send.at[kind, e, q], part_recv.at[kind, e, q],
+                )
+                chunks.append((job, kind, e, q))
+    links = [0 if bit < max(1, group_bits // 2) else 1 for bit in range(group_bits)]
+    events = plan([chunk[0].order for chunk in chunks], groups, links, 2)
 
     def weight_grads(kind, source):
         at = kind * experts_here * hidden_units
-        orders = [[second if e == 0 and q == 0 else first for q in range(PARTS)]
-                  for e in range(experts_here)]
+        orders = {(e, q): job.order for job, kind_of, e, q in chunks if kind_of == kind}
 
         def one(owner, _):
             columns = pl.ds(pl.multiple_of(owner * owned, LANES), owned)
@@ -196,22 +276,17 @@
             total = contract(left, right, ((0,), (0,))).astype(jnp.bfloat16)
             for e in range(experts_here):
                 for q in range(PARTS):
-                    parts[kind, e, q, position(owner, orders[e][q])] = total[
+                    parts[kind, e, q, position(owner, orders[e, q])] = total[
                         q * part_rows:(q + 1) * part_rows, e * hidden_units:(e + 1) * hidden_units
                     ]
             return 0
 
         lax.fori_loop(0, groups, one, 0)
-        for e in range(experts_here):
-            for q in range(PARTS):
-                job = Halving(
-                    "dp", orders[e][q], parts.at[kind, e, q], parts_recv.at[kind, e, q],
-                    part_send.at[kind, e, q], part_recv.at[kind, e, q],
-                )
-                job.start(0)
-                chunks.append((job, kind, e, q))
-
     weight_grads(2, c_buf)
+    early = [event for event in events if not event[0]][:3]
+    early = [event for event in early if chunks[event[1]][1] == 2]
+    for _, j, _ in early:
+        chunks[j][0].start(0)
     for bit in range(rank_bits):
         pl.semaphore_signal(
             ready.at[bit], 1, device_id={"expert": flipped(me, bit)}, device_id_type=MESH
@@ -243,20 +318,29 @@
     score_job.start(0)
 
     outs = (gate_out, up_out, down_out)
-    for turn in range(len(chunks) + group_bits - 1):
-        for stage in range(group_bits):
-            if 0 <= turn - stage < len(chunks):
-                job, kind, e, q = chunks[turn - stage]
-                total = job.step(stage)
-                if total is not None:
-                    outs[kind][e, q * part_rows:(q + 1) * part_rows, :] = total
-        if turn < rank_bits:
-            total = token_job.step(turn)
+    turn = 0
+    for event in events:
+        is_step, j, stage = event
+        job, kind, e, q = chunks[j]
+        if not is_step:
+            if event not in early:
+                job.start(0)
+            continue
+        total = job.step(stage)
+        if total is not None:
+            outs[kind][e, q * part_rows:(q + 1) * part_rows, :] = total.astype(jnp.bfloat16)
+        if turn % 4 == 3 and turn // 4 < rank_bits:
+            total = token_job.step(turn // 4)
             if total is not None:
                 tok_out[...] = total.astype(jnp.bfloat16)
-            total = score_job.step(turn)
+            total = score_job.step(turn // 4)
             if total is not None:
-                score_out[...] = total.astype(jnp.bfloat16)
+                total = total.T
+                for k in range(top):
+                    picked = jnp.where(named[k], total, 0.0)
+                    grads = jnp.sum(picked, axis=0, keepdims=True)
+                    score_out[k:k + 1, :] = grads.astype(jnp.bfloat16)
+        turn += 1
     for job in [chunk[0] for chunk in chunks] + [token_job, score_job]:
         job.finish()
 
@@ -265,37 +349,34 @@
     rows, width = tokens.shape
     experts_here, _, hidden_units = gate_weight.shape
     owned = width // groups
-    lane = jnp.arange(LANES, dtype=jnp.int32)
-    named = routes[:, :, None] == lane
-    dense = jnp.sum(jnp.where(named, combine[:, :, None].astype(jnp.float32), 0.0), axis=1)
-    dense = dense.astype(jnp.bfloat16)
     rank_bits, group_bits = ranks.bit_length() - 1, groups.bit_length() - 1
     bf16, dma = jnp.bfloat16, pltpu.SemaphoreType.DMA
     anywhere = pl.BlockSpec(memory_space=pl.ANY)
     vmem = pl.BlockSpec(memory_space=pltpu.VMEM)
-    grad = jax.ShapeDtypeStruct((experts_here, owned, hidden_units), jnp.float32)
+    grad = jax.ShapeDtypeStruct((experts_here, owned, hidden_units), bf16)
     chunk = (3, experts_here, PARTS)
     block = (owned // PARTS, hidden_units)
     token_grads, scores, gate_grads, up_grads, down_grads = pl.pallas_call(
         functools.partial(kernel, ranks, groups),
         out_shape=(
             jax.ShapeDtypeStruct((rows, width), bf16),
-            jax.ShapeDtypeStruct((rows, LANES), bf16),
+            jax.ShapeDtypeStruct(routes.shape[::-1], bf16),
             grad, grad, grad,
         ),
-        in_specs=[anywhere] * 6,
+        in_specs=[vmem] * 2 + [anywhere] * 5,
         out_specs=(vmem,) * 5,
         scratch_shapes=[
             pltpu.VMEM((ranks, rows, width), bf16),
             pltpu.VMEM((ranks, rows, width), bf16),
             pltpu.VMEM((ranks, rows, LANES), bf16),
+            pltpu.VMEM((2, experts_here, 2 * rows, hidden_units), jnp.float32),
             pltpu.VMEM((3,) + gate_weight.shape, bf16),
             pltpu.VMEM((ranks, rows, 3 * experts_here * hidden_units), bf16),
             pltpu.VMEM(chunk + (groups,) + block, bf16),
             pltpu.VMEM(chunk + (groups - 1,) + block, bf16),
             pltpu.VMEM((ranks, rows, LANES), bf16),
             pltpu.VMEM((ranks, rows, LANES), bf16),
-            dma((6,)),
+            dma((5,)),
             dma((ranks, 3)),
             dma((ranks, 3)),
             dma(chunk + (group_bits,)),
@@ -309,10 +390,9 @@
         compiler_params=pltpu.CompilerParams(
             collective_id=0, has_side_effects=True, vmem_limit_bytes=62 * 2**20
         ),
-    )(tokens, out_cotangent, dense, gate_weight, up_weight, down_weight)
-    picked = jnp.where(named, scores[:, None, :].astype(jnp.float32), 0.0)
-    combine_grads = jnp.sum(picked, axis=2).astype(bf16)
-    return token_grads, combine_grads, gate_grads, up_grads, down_grads
+    )(routes.T, combine.T, tokens, out_cotangent, gate_weight, up_weight, down_weight)
+    weight_grads = tuple(x.astype(jnp.float32) for x in (gate_grads, up_grads, down_grads))
+    return (token_grads, scores.T) + weight_grads
 
 
 def solution(mesh):

time: 196 us -> 173 us (0.88)
  Pallas kernels: 186 us -> 164 us
  local copies, waits for them, and re-layouts: 5.71 us -> 1.36 us
    pallas_call x1, Pallas kernels: 186 us -> 164 us  [local(): pl.pallas_call(functools.partial(kernel, ranks, groups), out_shape=(jax.S...]
    unnamed x10 -> x6, local copies, waits for them, and re-layouts: 5.71 us -> 1.36 us
    convert_element_type x2 -> x3, other arithmetic: 1.56 us -> 5.83 us  [local(): x.astype(jnp.float32)]
    reduce_sum x2 -> x0, other arithmetic: 2.32 us -> none  [the longest x1 1.51 us: local(): jnp.sum(jnp.where(named, combine[:, :, None].astype(jnp.float32), 0.0), a...]
where the time goes in v2:
time: 173 us; the launch traced here: 172 us
  Pallas kernels  164 us (95%)
  other arithmetic  5.83 us (3%)
    pallas_call x1, Pallas kernels, local(): pl.pallas_call(functools.partial(kernel, ranks, groups), out_shape=(jax.S...  164 us
    convert_element_type x3, other arithmetic, local(): x.astype(jnp.float32)  5.83 us

profile of v2, /device:TPU:0, one launch (start us, length us, event | category | flops | bytes accessed | tf_op | source)
XLA Modules:
  0.0 172.3 jit_solution(16588815880446199086)
XLA Ops:
  0.6 164.4 %shard_map.110 = (bf16[128,2048]{1,0:T(8,128)(2,1)}, bf16[4,128]{1,0:T(4,128)(2,1)}, bf16[2,256,384]{2,1,0:T(8,128)(2,1)}, bf16[2,256,384]{2,1,0:T(8,128)(2,1)}, bf16[2,256,384]{2,1,0:T(8,128)(2,1)}) custom-call(s32[4,128]{1,0:T(4,128)} %bitcast.3, bf16[4,128]{1,0:T(4,128)(2,1)} %bitcast.4, bf16[128,2048]{1,0:T(8,128)(2,1)} %tok_hbm.1, ...), custom_call_target="tpu_custom_call" | custom-call | tf_op jit(solution)/shard_map/pallas_call | solution.py:359
  165.0 0.0 copy-start
  165.0 0.0 copy-start.1
  165.1 2.0 %convert_element_type.9 = f32[2,256,384]{2,1,0:T(8,128)} convert(bf16[2,256,384]{2,1,0:T(8,128)(2,1)} %get-tuple-element.12) | non-fusion elementwise | flops 196608 | bytes 1179648 | tf_op jit(solution)/shard_map/convert_element_type | solution.py:394
  167.0 1.9 %convert_element_type.10 = f32[2,256,384]{2,1,0:T(8,128)} convert(bf16[2,256,384]{2,1,0:T(8,128)(2,1)} %get-tuple-element.13) | non-fusion elementwise | flops 196608 | bytes 1179648 | tf_op jit(solution)/shard_map/convert_element_type | solution.py:394
  169.0 1.9 %convert_element_type.11 = f32[2,256,384]{2,1,0:T(8,128)} convert(bf16[2,256,384]{2,1,0:T(8,128)(2,1)} %get-tuple-element.14) | non-fusion elementwise | flops 196608 | bytes 1179648 | tf_op jit(solution)/shard_map/convert_element_type | solution.py:394
  170.9 0.0 copy-done
  170.9 0.8 copy.14
  171.7 0.0 copy-done.1
  171.7 0.6 copy.15
Async XLA Ops:
  165.0 5.9 %copy-start = (bf16[128,2048]{1,0:T(8,128)(2,1)S(1)}, bf16[128,2048]{1,0:T(8,128)(2,1)}, u32[]{:S(2)}) copy-start(bf16[128,2048]{1,0:T(8,128)(2,1)} %get-tuple-element.20) | copy-start | bytes 1572868
  165.0 6.6 %copy-start.1 = (bf16[4,128]{1,0:T(4,128)(2,1)S(1)}, bf16[4,128]{1,0:T(4,128)(2,1)}, u32[]{:S(2)}) copy-start(bf16[4,128]{1,0:T(4,128)(2,1)} %get-tuple-element.11) | copy-start | bytes 3076

commit v3 on v2

--- a/solution.py
+++ b/solution.py
@@ -262,7 +262,7 @@
                 )
                 chunks.append((job, kind, e, q))
     links = [0 if bit < max(1, group_bits // 2) else 1 for bit in range(group_bits)]
-    events = plan([chunk[0].order for chunk in chunks], groups, links, 2)
+    events = plan([chunk[0].order for chunk in chunks], groups, links, 3)
 
     def weight_grads(kind, source):
         at = kind * experts_here * hidden_units
@@ -283,16 +283,10 @@
 
         lax.fori_loop(0, groups, one, 0)
     weight_grads(2, c_buf)
-    early = [event for event in events if not event[0]][:3]
-    early = [event for event in early if chunks[event[1]][1] == 2]
-    for _, j, _ in early:
-        chunks[j][0].start(0)
     for bit in range(rank_bits):
         pl.semaphore_signal(
             ready.at[bit], 1, device_id={"expert": flipped(me, bit)}, device_id_type=MESH
         )
-    weight_grads(0, x_buf)
-    weight_grads(1, x_buf)
 
     def token_part(step, _):
         strip = 2 * LANES
@@ -308,28 +302,31 @@
             x_buf[position(r, range(rank_bits)), :, columns] = total[r * rows:(r + 1) * rows]
         return 0
 
-    lax.fori_loop(0, width // (2 * LANES), token_part, 0)
     order = list(range(rank_bits))
     token_job = Halving("expert", order, x_buf, c_buf, tok_send, tok_recv)
     score_job = Halving("expert", order, score, score_recv, score_send, score_recv_sem)
-    for bit in range(rank_bits):
-        pl.semaphore_wait(ready.at[bit], 1)
-    token_job.start(0)
-    score_job.start(0)
-
     outs = (gate_out, up_out, down_out)
+    computed = {2}
     turn = 0
-    for event in events:
-        is_step, j, stage = event
+    for is_step, j, stage in events:
         job, kind, e, q = chunks[j]
+        if kind not in computed:
+            weight_grads(kind, x_buf)
+            computed.add(kind)
+            if len(computed) == 3:
+                lax.fori_loop(0, width // (2 * LANES), token_part, 0)
+                for bit in range(rank_bits):
+                    pl.semaphore_wait(ready.at[bit], 1)
+                token_job.start(0)
+                score_job.start(0)
+                turn = 0
         if not is_step:
-            if event not in early:
-                job.start(0)
+            job.start(0)
             continue
         total = job.step(stage)
         if total is not None:
-            outs[kind][e, q * part_rows:(q + 1) * part_rows, :] = total.astype(jnp.bfloat16)
-        if turn % 4 == 3 and turn // 4 < rank_bits:
+            outs[kind][e, q * part_rows:(q + 1) * part_rows, :] = total
+        if len(computed) == 3 and turn % 4 == 3 and turn // 4 < rank_bits:
             total = token_job.step(turn // 4)
             if total is not None:
                 tok_out[...] = total.astype(jnp.bfloat16)
@@ -345,6 +342,17 @@
         job.finish()
 
 
+def store(*refs):
+    count = len(refs) // 2
+    copies = [
+        pltpu.make_async_copy(refs[i], refs[count + i], refs[-1].at[i]) for i in range(count)
+    ]
+    for copy in copies:
+        copy.start()
+    for copy in copies:
+        copy.wait()
+
+
 def local(ranks, groups, tokens, routes, combine, out_cotangent, gate_weight, up_weight, down_weight):
     rows, width = tokens.shape
     experts_here, _, hidden_units = gate_weight.shape
@@ -353,10 +361,10 @@
     bf16, dma = jnp.bfloat16, pltpu.SemaphoreType.DMA
     anywhere = pl.BlockSpec(memory_space=pl.ANY)
     vmem = pl.BlockSpec(memory_space=pltpu.VMEM)
-    grad = jax.ShapeDtypeStruct((experts_here, owned, hidden_units), bf16)
+    grad = jax.ShapeDtypeStruct((experts_here, owned, hidden_units), jnp.float32)
     chunk = (3, experts_here, PARTS)
     block = (owned // PARTS, hidden_units)
-    token_grads, scores, gate_grads, up_grads, down_grads = pl.pallas_call(
+    results = pl.pallas_call(
         functools.partial(kernel, ranks, groups),
         out_shape=(
             jax.ShapeDtypeStruct((rows, width), bf16),
@@ -391,8 +399,16 @@
             collective_id=0, has_side_effects=True, vmem_limit_bytes=62 * 2**20
         ),
     )(routes.T, combine.T, tokens, out_cotangent, gate_weight, up_weight, down_weight)
-    weight_grads = tuple(x.astype(jnp.float32) for x in (gate_grads, up_grads, down_grads))
-    return (token_grads, scores.T) + weight_grads
+    results = pl.pallas_call(
+        store,
+        out_shape=tuple(jax.ShapeDtypeStruct(x.shape, x.dtype) for x in results),
+        in_specs=[anywhere] * len(results),
+        out_specs=(anywhere,) * len(results),
+        scratch_shapes=[dma((len(results),))],
+        compiler_params=pltpu.CompilerParams(vmem_limit_bytes=62 * 2**20),
+    )(*results)
+    token_grads, scores, gate_grads, up_grads, down_grads = results
+    return token_grads, scores.T, gate_grads, up_grads, down_grads
 
 
 def solution(mesh):

time: 173 us -> 257 us (1.49)
  Pallas kernels: 164 us -> 255 us
  other arithmetic: 5.83 us -> 0 us
    pallas_call x0 -> x1, Pallas kernels: none -> 88.5 us  [local(): pl.pallas_call(store, out_shape=tuple((jax.ShapeDtypeStruct(x.shape, x.dt...]
    convert_element_type x3 -> x0, other arithmetic: 5.83 us -> none  [local(): x.astype(jnp.float32)]
where the time goes in v3:
time: 257 us; the launch traced here: 256 us
  Pallas kernels  255 us (99%)
    pallas_call x1, Pallas kernels, local(): pl.pallas_call(functools.partial(kernel, ranks, groups), out_shape=(jax.S...  167 us
    pallas_call x1, Pallas kernels, local(): pl.pallas_call(store, out_shape=tuple((jax.ShapeDtypeStruct(x.shape, x.dt...  88.5 us

profile of v3, /device:TPU:0, one launch (start us, length us, event | category | flops | bytes accessed | tf_op | source)
XLA Modules:
  0.0 256.0 jit_solution(8436618746918175106)
XLA Ops:
  0.6 166.7 %shard_map.110 = (bf16[128,2048]{1,0:T(8,128)(2,1)}, bf16[4,128]{1,0:T(4,128)(2,1)}, f32[2,256,384]{2,1,0:T(8,128)}, f32[2,256,384]{2,1,0:T(8,128)}, f32[2,256,384]{2,1,0:T(8,128)}) custom-call(s32[4,128]{1,0:T(4,128)} %bitcast.3, bf16[4,128]{1,0:T(4,128)(2,1)} %bitcast.4, bf16[128,2048]{1,0:T(8,128)(2,1)} %tok_hbm.1, bf16[128,2048]{1,0:T(8,128)(2,1)} %cot_hbm.1, ...), custom_call_target="tpu_custom_call" | custom-call | tf_op jit(solution)/shard_map/pallas_call | solution.py:367
  167.3 88.5 %shard_map.111 = (bf16[128,2048]{1,0:T(8,128)(2,1)}, bf16[4,128]{1,0:T(4,128)(2,1)}, f32[2,256,384]{2,1,0:T(8,128)}, f32[2,256,384]{2,1,0:T(8,128)}, f32[2,256,384]{2,1,0:T(8,128)}) custom-call(bf16[128,2048]{1,0:T(8,128)(2,1)} %get-tuple-element.15.refs_0_, bf16[4,128]{1,0:T(4,128)(2,1)} %get-tuple-element.16.refs_1_, ...), custom_call_target="tpu_custom_call" | custom-call | tf_op jit(solution)/shard_map/pallas_call | solution.py:402

commit v4 on v2

--- a/solution.py
+++ b/solution.py
@@ -9,7 +9,7 @@
 
 MESH = pl.DeviceIdType.MESH
 LANES = 128
-PARTS = 2
+PARTS = 4
 
 
 def bit_of(index, bit):
@@ -250,7 +250,7 @@
 
     first = list(range(group_bits))
     second = [1, 0] + first[2:] if group_bits > 1 else first
-    second_at = [(e, q) for e in range(experts_here) for q in range(PARTS)][:1]
+    second_at = [(e, 0) for e in range(experts_here)]
     chunks = []
     for kind in (2, 0, 1):
         for e in range(experts_here):
@@ -262,7 +262,7 @@
                 )
                 chunks.append((job, kind, e, q))
     links = [0 if bit < max(1, group_bits // 2) else 1 for bit in range(group_bits)]
-    events = plan([chunk[0].order for chunk in chunks], groups, links, 2)
+    events = plan([chunk[0].order for chunk in chunks], groups, links, 3)
 
     def weight_grads(kind, source):
         at = kind * experts_here * hidden_units
@@ -283,7 +283,7 @@
 
         lax.fori_loop(0, groups, one, 0)
     weight_grads(2, c_buf)
-    early = [event for event in events if not event[0]][:3]
+    early = [event for event in events if not event[0]][:6]
     early = [event for event in early if chunks[event[1]][1] == 2]
     for _, j, _ in early:
         chunks[j][0].start(0)
@@ -328,12 +328,12 @@
             continue
         total = job.step(stage)
         if total is not None:
-            outs[kind][e, q * part_rows:(q + 1) * part_rows, :] = total.astype(jnp.bfloat16)
-        if turn % 4 == 3 and turn // 4 < rank_bits:
-            total = token_job.step(turn // 4)
+            outs[kind][e, q * part_rows:(q + 1) * part_rows, :] = total
+        if turn % 8 == 7 and turn // 8 < rank_bits:
+            total = token_job.step(turn // 8)
             if total is not None:
                 tok_out[...] = total.astype(jnp.bfloat16)
-            total = score_job.step(turn // 4)
+            total = score_job.step(turn // 8)
             if total is not None:
                 total = total.T
                 for k in range(top):
@@ -345,6 +345,17 @@
         job.finish()
 
 
+def store(*refs):
+    count = len(refs) // 2
+    copies = [
+        pltpu.make_async_copy(refs[i], refs[count + i], refs[-1].at[i]) for i in range(count)
+    ]
+    for copy in copies:
+        copy.start()
+    for copy in copies:
+        copy.wait()
+
+
 def local(ranks, groups, tokens, routes, combine, out_cotangent, gate_weight, up_weight, down_weight):
     rows, width = tokens.shape
     experts_here, _, hidden_units = gate_weight.shape
@@ -353,10 +364,10 @@
     bf16, dma = jnp.bfloat16, pltpu.SemaphoreType.DMA
     anywhere = pl.BlockSpec(memory_space=pl.ANY)
     vmem = pl.BlockSpec(memory_space=pltpu.VMEM)
-    grad = jax.ShapeDtypeStruct((experts_here, owned, hidden_units), bf16)
+    grad = jax.ShapeDtypeStruct((experts_here, owned, hidden_units), jnp.float32)
     chunk = (3, experts_here, PARTS)
     block = (owned // PARTS, hidden_units)
-    token_grads, scores, gate_grads, up_grads, down_grads = pl.pallas_call(
+    results = pl.pallas_call(
         functools.partial(kernel, ranks, groups),
         out_shape=(
             jax.ShapeDtypeStruct((rows, width), bf16),
@@ -391,8 +402,15 @@
             collective_id=0, has_side_effects=True, vmem_limit_bytes=62 * 2**20
         ),
     )(routes.T, combine.T, tokens, out_cotangent, gate_weight, up_weight, down_weight)
-    weight_grads = tuple(x.astype(jnp.float32) for x in (gate_grads, up_grads, down_grads))
-    return (token_grads, scores.T) + weight_grads
+    results = pl.pallas_call(
+        store,
+        out_shape=tuple(jax.ShapeDtypeStruct(x.shape, x.dtype) for x in results),
+        in_specs=[vmem] * len(results),
+        out_specs=(anywhere,) * len(results),
+        scratch_shapes=[dma((len(results),))],
+    )(*results)
+    token_grads, scores, gate_grads, up_grads, down_grads = results
+    return token_grads, scores.T, gate_grads, up_grads, down_grads
 
 
 def solution(mesh):

time: 173 us -> 188 us (1.087)
  Pallas kernels: 164 us -> 186 us
  other arithmetic: 5.83 us -> 0 us
    pallas_call x1, Pallas kernels: 164 us -> 183 us  [local(): pl.pallas_call(functools.partial(kernel, ranks, groups), out_shape=(jax.S...]
    convert_element_type x3 -> x0, other arithmetic: 5.83 us -> none  [local(): x.astype(jnp.float32)]
    pallas_call x0 -> x1, Pallas kernels: none -> 3.39 us  [local(): pl.pallas_call(store, out_shape=tuple((jax.ShapeDtypeStruct(x.shape, x.dt...]
where the time goes in v4:
time: 188 us; the launch traced here: 187 us
  Pallas kernels  186 us (99%)
    pallas_call x1, Pallas kernels, local(): pl.pallas_call(functools.partial(kernel, ranks, groups), out_shape=(jax.S...  183 us

profile of v4, /device:TPU:0, one launch (start us, length us, event | category | flops | bytes accessed | tf_op | source)
XLA Modules:
  0.0 186.7 jit_solution(187768187479817369)
XLA Ops:
  0.6 182.5 %shard_map.110 = (bf16[128,2048]{1,0:T(8,128)(2,1)}, bf16[4,128]{1,0:T(4,128)(2,1)}, f32[2,256,384]{2,1,0:T(8,128)}, f32[2,256,384]{2,1,0:T(8,128)}, f32[2,256,384]{2,1,0:T(8,128)}) custom-call(s32[4,128]{1,0:T(4,128)} %bitcast.3, bf16[4,128]{1,0:T(4,128)(2,1)} %bitcast.4, bf16[128,2048]{1,0:T(8,128)(2,1)} %tok_hbm.1, bf16[128,2048]{1,0:T(8,128)(2,1)} %cot_hbm.1, ...), custom_call_target="tpu_custom_call" | custom-call | tf_op jit(solution)/shard_map/pallas_call | solution.py:370
  183.2 3.4 %shard_map.111 = (bf16[128,2048]{1,0:T(8,128)(2,1)}, bf16[4,128]{1,0:T(4,128)(2,1)}, f32[2,256,384]{2,1,0:T(8,128)}, f32[2,256,384]{2,1,0:T(8,128)}, f32[2,256,384]{2,1,0:T(8,128)}) custom-call(bf16[128,2048]{1,0:T(8,128)(2,1)} %get-tuple-element.15.refs_0_, bf16[4,128]{1,0:T(4,128)(2,1)} %get-tuple-element.16.refs_1_, ...), custom_call_target="tpu_custom_call" | custom-call | tf_op jit(solution)/shard_map/pallas_call | solution.py:405
